TPU v7x, 128 devices: a whole 4x4x4 slice. The times are simulated.
128 devices in a mesh: row: 16 (over x_hi, y, core), col: 8 (over z, x_lo).
Axes of the slice: x: 4 (x_hi: 2, x_lo: 2; x = x_hi * 2 + x_lo), y: 4, z: 4, core: 2. Of those that a mesh axis runs over, the one named last changes fastest.
Arguments:
- tokens: bfloat16 [16384, 2048], P(('row', 'col')), may hold values from -6 to 6
- doc_lengths: int32 [16, 3], P('row'), may hold values from 0 to 1024, as said below
- input_gain: bfloat16 [2048], replicated, may hold values from 0.25 to 1.75
- input_shift: bfloat16 [2048], replicated, may hold values from -1.75 to 1.75
- post_gain: bfloat16 [2048], replicated, may hold values from 0.25 to 1.75
- post_shift: bfloat16 [2048], replicated, may hold values from -1.75 to 1.75
- qkv_weight: bfloat16 [2048, 6144], P('row', 'col'), may hold values from -0.125 to 0.125
- qkv_bias: bfloat16 [6144], P(('col', 'row')), may hold values from -1.75 to 1.75
- dense_weight: bfloat16 [2048, 2048], P('col', 'row'), may hold values from -1 to 1
- dense_bias: bfloat16 [2048], replicated, may hold values from -1.75 to 1.75
- up_weight: bfloat16 [2048, 8192], P('row', 'col'), may hold values from -0.125 to 0.125
- up_bias: bfloat16 [8192], P(('col', 'row')), may hold values from -3 to 3
- down_weight: bfloat16 [8192, 2048], P('col', 'row'), may hold values from -0.0625 to 0.0625
- down_bias: bfloat16 [2048], replicated, may hold values from -1.75 to 1.75
- cotangent: bfloat16 [16384, 2048], P(('row', 'col')), may hold values from -6 to 6
Outputs:
- layer_out: bfloat16 [16384, 2048], P(('row', 'col'))
- input_grad: bfloat16 [16384, 2048], P(('row', 'col'))
- input_gain_grad: float32 [2048], replicated
- input_shift_grad: float32 [2048], replicated
- post_gain_grad: float32 [2048], replicated
- post_shift_grad: float32 [2048], replicated
- qkv_weight_grad: float32 [2048, 6144], P('row', 'col')
- qkv_bias_grad: float32 [6144], P(('col', 'row'))
- dense_weight_grad: float32 [2048, 2048], P('col', 'row')
- dense_bias_grad: float32 [2048], replicated
- up_weight_grad: float32 [2048, 8192], P('row', 'col')
- up_bias_grad: float32 [8192], P(('col', 'row'))
- down_weight_grad: float32 [8192, 2048], P('col', 'row')
- down_bias_grad: float32 [2048], replicated
Inputs may be any that keep to these rules, and one draw needn't show every extreme that they name: `doc_lengths`: each row lists the 3 documents of one group of 1024 tokens in order and sums to 1024; a zero is an empty document. In every row one document begins within the group's first 128 tokens and ends within its last 128.
All inputs are finite; a program needn't handle non-finite values.
Results may differ from a plain program's by a relative error of at most 0.023.
Values may be sent and summed in bfloat16 or wider, within the bound.
No kernel may reach another device: no remote copies, remote signals or barrier semaphores. Data moves between devices by JAX's collectives and lax.ppermute only.
A program may use at most 128 MiB of HBM per device.

v0:
```python
import math

import jax
import jax.numpy as jnp
from jax import lax
from jax.sharding import PartitionSpec as P

HS = 256
ROT = 64


def layer_norm(tok_rows, gain, shift):
    center_mean = jnp.mean(tok_rows, axis=-1, keepdims=True)
    centered = tok_rows - center_mean
    variance = jnp.mean(centered * centered, axis=-1, keepdims=True)
    return centered * lax.rsqrt(variance + 1e-05) * gain + shift


def both_norms(tok_rows, gain_one, shift_one, gain_two, shift_two):
    return (layer_norm(tok_rows, gain_one, shift_one), layer_norm(tok_rows, gain_two, shift_two))


def doc_layout(lengths, row_count):
    ends = jnp.cumsum(lengths, dtype=jnp.int32)
    places = jnp.arange(row_count, dtype=jnp.int32)
    passed = places[:, None] >= ends[None, :]
    doc_ids = jnp.sum(passed.astype(jnp.int32), axis=1, dtype=jnp.int32)
    begins = jnp.sum(jnp.where(passed, lengths[None, :], 0), axis=1, dtype=jnp.int32)
    return (doc_ids, places - begins)


def rotary_tables(positions, width):
    half_width = width // 2
    frequency = 1.0 / 10000.0 ** (jnp.arange(half_width, dtype=jnp.float32) * (2.0 / width))
    angles = positions.astype(jnp.float32)[:, None] * frequency[None, :]
    return (jnp.cos(angles)[:, None, :], jnp.sin(angles)[:, None, :])


def rotate(portion, cosine, sine_part):
    half_width = cosine.shape[-1]
    lead_part = portion[..., :half_width]
    tail_part = portion[..., half_width : 2 * half_width]
    return jnp.concatenate(
        [
            lead_part * cosine - tail_part * sine_part,
            tail_part * cosine + lead_part * sine_part,
            portion[..., 2 * half_width :],
        ],
        axis=-1,
    )


def gelu_exact(values):
    return 0.5 * values * (1.0 + lax.erf(values * (1.0 / math.sqrt(2.0))))


def inner_rows(left, right):
    return lax.dot_general(
        left, right, (((0,), (0,)), ((), ())), preferred_element_type=jnp.float32
    )


def outer_cols(left, right):
    return lax.dot_general(
        left, right, (((1,), (1,)), ((), ())), preferred_element_type=jnp.float32
    )


def block_mask(doc_ids, offset, block_rows):
    row_count = doc_ids.shape[0]
    places = jnp.arange(row_count, dtype=jnp.int32)
    block_places = offset + jnp.arange(block_rows, dtype=jnp.int32)
    block_docs = lax.dynamic_slice_in_dim(doc_ids, offset, block_rows, 0)
    return (block_docs[:, None] == doc_ids[None, :]) & (places[None, :] <= block_places[:, None])


def attend_forward(queries, key_rows, values, doc_ids, block_rows):
    row_count = queries.shape[0]
    scaling = HS ** (-0.5)

    def one_block(offset):
        block_query = lax.dynamic_slice_in_dim(queries, offset, block_rows, 0)
        allowed = block_mask(doc_ids, offset, block_rows)
        scores = (
            jnp.einsum("qhe,khe->hqk", block_query, key_rows, preferred_element_type=jnp.float32)
            * scaling
        )
        scores = jnp.where(allowed[None], scores, -1e30)
        row_max = jnp.max(scores, axis=-1, keepdims=True)
        raised = jnp.exp(scores - row_max)
        totals = jnp.sum(raised, axis=-1, keepdims=True)
        probabilities = (raised / totals).astype(jnp.bfloat16)
        outcome = jnp.einsum(
            "hqk,khe->qhe", probabilities, values, preferred_element_type=jnp.float32
        )
        return (outcome.astype(jnp.bfloat16), (row_max + jnp.log(totals))[..., 0])

    offsets = jnp.arange(row_count // block_rows, dtype=jnp.int32) * block_rows
    outcome, log_totals = lax.map(one_block, offsets)
    return (outcome.reshape(row_count, -1), log_totals)


def attend_backward(queries, key_rows, values, doc_ids, log_totals, d_attended, block_rows):
    row_count = queries.shape[0]
    scaling = HS ** (-0.5)

    def one_block(carry, packed):
        offset, block_log = packed
        d_keys, d_values = carry
        block_query = lax.dynamic_slice_in_dim(queries, offset, block_rows, 0)
        block_grad = lax.dynamic_slice_in_dim(d_attended, offset, block_rows, 0)
        allowed = block_mask(doc_ids, offset, block_rows)
        scores = (
            jnp.einsum("qhe,khe->hqk", block_query, key_rows, preferred_element_type=jnp.float32)
            * scaling
        )
        scores = jnp.where(allowed[None], scores, -1e30)
        soft_weights = jnp.exp(scores - block_log[..., None])
        probabilities = soft_weights.astype(jnp.bfloat16)
        d_probs = jnp.einsum("qhe,khe->hqk", block_grad, values, preferred_element_type=jnp.float32)
        inner_sum = jnp.sum(soft_weights * d_probs, axis=-1, keepdims=True)
        d_scores = (soft_weights * (d_probs - inner_sum)).astype(jnp.bfloat16)
        d_values = d_values + jnp.einsum(
            "hqk,qhe->khe", probabilities, block_grad, preferred_element_type=jnp.float32
        )
        d_keys = (
            d_keys
            + jnp.einsum("hqk,qhe->khe", d_scores, block_query, preferred_element_type=jnp.float32)
            * scaling
        )
        d_block = (
            jnp.einsum("hqk,khe->qhe", d_scores, key_rows, preferred_element_type=jnp.float32)
            * scaling
        )
        return ((d_keys, d_values), d_block)

    offsets = jnp.arange(row_count // block_rows, dtype=jnp.int32) * block_rows
    zero_grads = jnp.zeros(key_rows.shape, jnp.float32)
    (d_keys, d_values), d_queries = lax.scan(
        one_block, (zero_grads, zero_grads), (offsets, log_totals)
    )
    return (d_queries.reshape(queries.shape), d_keys, d_values)


def shards(
    tokens,
    doc_lengths,
    input_gain,
    input_shift,
    post_gain,
    post_shift,
    qkv_weight,
    qkv_bias,
    dense_weight,
    dense_bias,
    up_weight,
    up_bias,
    down_weight,
    down_bias,
    cotangent,
):
    tok_rows = tokens.astype(jnp.float32)
    norm_params = (
        input_gain.astype(jnp.float32),
        input_shift.astype(jnp.float32),
        post_gain.astype(jnp.float32),
        post_shift.astype(jnp.float32),
    )
    normed, norm_back = jax.vjp(
        both_norms, tok_rows, norm_params[0], norm_params[1], norm_params[2], norm_params[3]
    )
    first_norm, second_norm = (
        lax.all_gather(normed[0].astype(jnp.bfloat16), "col", axis=0, tiled=True),
        lax.all_gather(normed[1].astype(jnp.bfloat16), "col", axis=0, tiled=True),
    )
    qkv_full, qkv_bias_full, up_full, up_bias_full, dense_full, down_full = (
        lax.all_gather(qkv_weight, "row", axis=0, tiled=True),
        lax.all_gather(qkv_bias, "row", axis=0, tiled=True),
        lax.all_gather(up_weight, "row", axis=0, tiled=True),
        lax.all_gather(up_bias, "row", axis=0, tiled=True),
        lax.all_gather(dense_weight, "row", axis=1, tiled=True),
        lax.all_gather(down_weight, "row", axis=1, tiled=True),
    )
    row_count = first_norm.shape[0]
    head_dev = dense_full.shape[0] // HS
    block_rows = min(512, row_count)
    doc_ids, positions = doc_layout(doc_lengths[0], row_count)
    cosine, sine_part = rotary_tables(positions, ROT)
    mixture = (
        jnp.dot(first_norm, qkv_full, preferred_element_type=jnp.float32)
        + qkv_bias_full.astype(jnp.float32)
    ).reshape(row_count, head_dev, 3, HS)
    queries = rotate(mixture[:, :, 0], cosine, sine_part).astype(jnp.bfloat16)
    key_rows = rotate(mixture[:, :, 1], cosine, sine_part).astype(jnp.bfloat16)
    values = mixture[:, :, 2].astype(jnp.bfloat16)
    attended, log_totals = attend_forward(queries, key_rows, values, doc_ids, block_rows)
    hidden = jnp.dot(
        second_norm, up_full, preferred_element_type=jnp.float32
    ) + up_bias_full.astype(jnp.float32)
    active = gelu_exact(hidden).astype(jnp.bfloat16)
    summed = lax.psum_scatter(
        (
            jnp.dot(attended, dense_full, preferred_element_type=jnp.float32)
            + jnp.dot(active, down_full, preferred_element_type=jnp.float32)
        ).astype(jnp.bfloat16),
        "col",
        scatter_dimension=0,
        tiled=True,
    ).astype(jnp.float32)
    layer_out = (
        tok_rows + summed + dense_bias.astype(jnp.float32) + down_bias.astype(jnp.float32)
    ).astype(jnp.bfloat16)
    grad_rows = lax.all_gather(cotangent, "col", axis=0, tiled=True)
    dense_back, down_back, qkv_back, up_back = (
        lax.all_gather(dense_weight, "row", axis=1, tiled=True),
        lax.all_gather(down_weight, "row", axis=1, tiled=True),
        lax.all_gather(qkv_weight, "row", axis=0, tiled=True),
        lax.all_gather(up_weight, "row", axis=0, tiled=True),
    )
    down_grad = inner_rows(active, grad_rows)
    d_active = outer_cols(grad_rows, down_back)
    d_hidden = jax.vjp(gelu_exact, hidden)[1](d_active)[0].astype(jnp.bfloat16)
    up_grad = inner_rows(second_norm, d_hidden)
    up_bias_grad = jnp.sum(d_hidden.astype(jnp.float32), axis=0)
    d_second = outer_cols(d_hidden, up_back)
    dense_grad = inner_rows(attended, grad_rows)
    d_attended = (
        outer_cols(grad_rows, dense_back).astype(jnp.bfloat16).reshape(row_count, head_dev, HS)
    )
    d_queries, d_keys, d_values = attend_backward(
        queries, key_rows, values, doc_ids, log_totals, d_attended, block_rows
    )
    d_mixture = jnp.stack(
        [rotate(d_queries, cosine, -sine_part), rotate(d_keys, cosine, -sine_part), d_values],
        axis=2,
    )
    d_mixture = d_mixture.reshape(row_count, head_dev * 3 * HS).astype(jnp.bfloat16)
    qkv_grad = inner_rows(first_norm, d_mixture)
    qkv_bias_grad = jnp.sum(d_mixture.astype(jnp.float32), axis=0)
    d_first = outer_cols(d_mixture, qkv_back)
    qkv_total, qkv_bias_total, up_total, up_bias_total, dense_total, down_total = (
        lax.psum_scatter(
            qkv_grad.astype(jnp.bfloat16), "row", scatter_dimension=0, tiled=True
        ).astype(jnp.float32),
        lax.psum_scatter(
            qkv_bias_grad.astype(jnp.bfloat16), "row", scatter_dimension=0, tiled=True
        ).astype(jnp.float32),
        lax.psum_scatter(
            up_grad.astype(jnp.bfloat16), "row", scatter_dimension=0, tiled=True
        ).astype(jnp.float32),
        lax.psum_scatter(
            up_bias_grad.astype(jnp.bfloat16), "row", scatter_dimension=0, tiled=True
        ).astype(jnp.float32),
        lax.psum_scatter(
            dense_grad.astype(jnp.bfloat16), "row", scatter_dimension=1, tiled=True
        ).astype(jnp.float32),
        lax.psum_scatter(
            down_grad.astype(jnp.bfloat16), "row", scatter_dimension=1, tiled=True
        ).astype(jnp.float32),
    )
    d_normed = (
        lax.psum_scatter(
            d_first.astype(jnp.bfloat16), "col", scatter_dimension=0, tiled=True
        ).astype(jnp.float32),
        lax.psum_scatter(
            d_second.astype(jnp.bfloat16), "col", scatter_dimension=0, tiled=True
        ).astype(jnp.float32),
    )
    d_tokens, gain_one, shift_one, gain_two, shift_two = norm_back((d_normed[0], d_normed[1]))
    input_grad = (cotangent.astype(jnp.float32) + d_tokens).astype(jnp.bfloat16)
    bias_grad = jnp.sum(cotangent.astype(jnp.float32), axis=0)
    small_sums = lax.psum((gain_one, shift_one, gain_two, shift_two, bias_grad), ("row", "col"))
    return (
        layer_out,
        input_grad,
        small_sums[0],
        small_sums[1],
        small_sums[2],
        small_sums[3],
        qkv_total,
        qkv_bias_total,
        dense_total,
        small_sums[4],
        up_total,
        up_bias_total,
        down_total,
        small_sums[4],
    )


def solution(mesh):
    return jax.shard_map(
        shards,
        mesh=mesh,
        in_specs=(
            P(("row", "col"), None),
            P("row", None),
            P(),
            P(),
            P(),
            P(),
            P("row", "col"),
            P(("col", "row")),
            P("col", "row"),
            P(),
            P("row", "col"),
            P(("col", "row")),
            P("col", "row"),
            P(),
            P(("row", "col"), None),
        ),
        out_specs=(
            P(("row", "col"), None),
            P(("row", "col"), None),
            P(),
            P(),
            P(),
            P(),
            P("row", "col"),
            P(("col", "row")),
            P("col", "row"),
            P(),
            P("row", "col"),
            P(("col", "row")),
            P("col", "row"),
            P(),
        ),
        check_vma=False,
    )
```

profile of v0, /device:TPU:1, one launch (start us, length us, event | category | flops | bytes accessed | tf_op | source)
XLA Modules:
  0.0 1171.6 jit_solution(3537268997468523561)
XLA Ops:
  22.3 34.4 %all-reduce.6 = (bf16[1024]{0:T(1024)(128)(2,1)S(1)}, bf16[768]{0:T(1024)(128)(2,1)S(1)}) all-reduce(bf16[1024]{0:T(1024)(128)(2,1)S(1)} %dynamic-update-slice.1, bf16[768]{0:T(1024)(128)(2,1)S(1)} %dynamic-update-slice), channel_id=1, replica_groups=mesh['row'=16,'col'=8] {'row'}, use_global_device_ids=true, to_apply=%add.1 | all-reduce | flops 1792 | bytes 7168
  56.8 8.1 all-gather.10.cloned.1.call-done
  64.9 91.3 %all-gather.8.cloned.1.call-done = bf16[1024,2048]{1,0:T(8,128)(2,1)} async-done(((bf16[128,2048]{1,0:T(8,128)(2,1)}), bf16[1024,2048]{1,0:T(8,128)(2,1)}) %all-gather.8.cloned.1.call-update) | async-done | bytes 4194320 | tf_op jit(solution)/shard_map/all_gather | solution.py:173
  168.7 32.9 %all-gather.12.cloned.1.call-done = bf16[256,2048]{1,0:T(8,128)(2,1)} async-done(((bf16[256,128]{1,0:T(8,128)(2,1)}), bf16[256,2048]{1,0:T(8,128)(2,1)}) %all-gather.12.cloned.1.call-update) | async-done | bytes 1048592 | tf_op jit(solution)/shard_map/all_gather | solution.py:181
  201.6 91.9 %all-gather.20.cloned.1.call-done = bf16[1024,2048]{1,0:T(8,128)(2,1)} async-done(((bf16[128,2048]{1,0:T(8,128)(2,1)}), bf16[1024,2048]{1,0:T(8,128)(2,1)}) %all-gather.20.cloned.1.call-update) | async-done | bytes 4194320 | tf_op jit(solution)/shard_map/all_gather | solution.py:213
  297.3 14.2 %while.27 = (s32[]{:T(128)}, bf16[2,512,1,256]{3,1,2,0:T(8,128)(2,1)}, f32[2,1,512]{2,1,0:T(1,128)S(1)}, s32[2]{0:T(128)S(1)}, s32[1024]{0:T(1024)S(1)}, /*index...) while((s32[]{:T(128)}, ...), condition=%wide.region_8.9_spmd, body=%wide.region_5.0_spmd.sunk | while | flops 542769152 | bytes 12093679 | solution.py:99
  311.5 18.2 %while.28 = (s32[]{:T(128)}, f32[1024,1,256]{0,2,1:T(8,128)S(1)}, f32[1024,1,256]{0,2,1:T(8,128)S(1)}, f32[2,512,1,256]{3,1,2,0:T(8,128)}, s32[2]{0:T(128)S(1)},...) while((s32[]{:T(128)}, f32[1024,1,256]{0,2,1:T(8,128)S(1)}, ...), condition=%wide.region_15.16_spmd.clone, body=%wide.region_13.15_spmd.clone.sunk | while | flops 1349910528 | bytes 35676500 | solution.py:139
  350.3 36.1 %all-gather.14.cloned.1.call-done = bf16[1024,2048]{1,0:T(8,128)(2,1)} async-done(((bf16[128,2048]{1,0:T(8,128)(2,1)}), bf16[1024,2048]{1,0:T(8,128)(2,1)}) %all-gather.14.cloned.1.call-update) | async-done | bytes 4194320 | tf_op jit(solution)/shard_map/all_gather | solution.py:174
  386.4 57.9 %all-gather.16.cloned.1.call-done = bf16[2048,1024]{1,0:T(8,128)(2,1)} async-done(((bf16[128,1024]{1,0:T(8,128)(2,1)}), bf16[2048,1024]{1,0:T(8,128)(2,1)}) %all-gather.16.cloned.1.call-update) | async-done | bytes 4194320 | tf_op jit(solution)/shard_map/all_gather | solution.py:179
  444.3 10.3 multiply_convert_fusion.1
  462.3 6.4 copy.68
  469.0 32.1 %all-gather.18.cloned.1.call-done = bf16[1024,2048]{1,0:T(8,128)(2,1)} async-done(((bf16[1024,128]{1,0:T(8,128)(2,1)}), bf16[1024,2048]{1,0:T(8,128)(2,1)}) %all-gather.18.cloned.1.call-update) | async-done | bytes 4194320 | tf_op jit(solution)/shard_map/all_gather | solution.py:182
  501.1 10.0 fusion.89
  518.8 7.0 convolution_convert_fusion.1
  527.4 8.3 convolution_convert_fusion.4
  536.0 7.1 fusion.94
  548.0 32.8 %all-reduce.5 = (bf16[768]{0:T(1024)(128)(2,1)S(1)}, bf16[1024]{0:T(1024)(128)(2,1)S(1)}) all-reduce(bf16[768]{0:T(1024)(128)(2,1)S(1)} %reduce_sum.186, bf16[1024]{0:T(1024)(128)(2,1)S(1)} %get-tuple-element.292), channel_id=6, replica_groups=mesh['row'=16,'col'=8] {'row'}, use_global_device_ids=true, to_apply=%region_29.30.clone | all-reduce | flops 1792 | bytes 7168
  583.5 63.3 %reduce-scatter.18.cloned.1.call-done = bf16[128,768]{1,0:T(8,128)(2,1)} async-done(((bf16[2048,768]{1,0:T(8,128)(2,1)}), bf16[128,768]{1,0:T(8,128)(2,1)}) %reduce-scatter.18.cloned.1.call-update) | async-done | bytes 196624 | tf_op jit(solution)/shard_map/reduce_scatter | solution.py:242
  648.6 81.8 %reduce-scatter.24.cloned.1.call-done = bf16[128,1024]{1,0:T(8,128)(2,1)} async-done(((bf16[2048,1024]{1,0:T(8,128)(2,1)}), bf16[128,1024]{1,0:T(8,128)(2,1)}) %reduce-scatter.24.cloned.1.call-update) | async-done | bytes 262160
  732.4 81.4 %reduce-scatter.20.cloned.1.call-done = bf16[128,1024]{1,0:T(8,128)(2,1)} async-done(((bf16[2048,1024]{1,0:T(8,128)(2,1)}), bf16[128,1024]{1,0:T(8,128)(2,1)}) %reduce-scatter.20.cloned.1.call-update) | async-done | bytes 262160 | tf_op jit(solution)/shard_map/reduce_scatter | solution.py:248
  815.6 92.1 %reduce-scatter.16.cloned.1.call-done = bf16[128,2048]{1,0:T(8,128)(2,1)} async-done(((bf16[1024,2048]{1,0:T(8,128)(2,1)}), bf16[128,2048]{1,0:T(8,128)(2,1)}) %reduce-scatter.16.cloned.1.call-update) | async-done | bytes 524304 | tf_op jit(solution)/shard_map/reduce_scatter | solution.py:262
  907.7 93.8 %reduce-scatter.14.cloned.1.call-done = bf16[128,2048]{1,0:T(8,128)(2,1)} async-done(((bf16[1024,2048]{1,0:T(8,128)(2,1)}), bf16[128,2048]{1,0:T(8,128)(2,1)}) %reduce-scatter.14.cloned.1.call-update) | async-done | bytes 524304 | tf_op jit(solution)/shard_map/reduce_scatter | solution.py:265
  1005.6 89.6 %reduce-scatter.12.cloned.1.call-done = bf16[128,2048]{1,0:T(8,128)(2,1)} async-done(((bf16[1024,2048]{1,0:T(8,128)(2,1)}), bf16[128,2048]{1,0:T(8,128)(2,1)}) %reduce-scatter.12.cloned.1.call-update) | async-done | bytes 524304 | tf_op jit(solution)/shard_map/reduce_scatter | solution.py:201
  1098.7 65.3 %all-reduce.4 = (f32[2048]{0:T(1024)}, f32[2048]{0:T(1024)}, f32[2048]{0:T(1024)}, f32[2048]{0:T(1024)}, f32[2048]{0:T(1024)S(1)}) all-reduce(f32[2048]{0:T(1024)S(1)} %get-tuple-element.238, f32[2048]{0:T(1024)S(1)} %get-tuple-element.241, f32[2048]{0:T(1024)S(1)} %get-tuple-element.233, ...), channel_id=1, replica_groups=mesh['row'=16,'col'=8] {'row','col'}, use_global_device_ids=true, to_apply=%region_20.21 | all-reduce | flops 10240 | bytes 81920 | tf_op jit(solution)/shard_map/psum | solution.py:272
  (217 shorter events, 111.9 us)
Async XLA Ops:
  7.2 14.5 %copy-start.25 = (s32[1,3]{1,0:T(1,128)S(1)}, s32[1,3]{1,0:T(1,128)}, u32[]{:S(2)}) copy-start(s32[1,3]{1,0:T(1,128)} %param.20) | copy-start | bytes 40
  7.2 14.7 %copy-start.29 = (bf16[48]{0:T(256)(128)(2,1)S(1)}, bf16[48]{0:T(256)(128)(2,1)}, u32[]{:S(2)}) copy-start(bf16[48]{0:T(256)(128)(2,1)} %param.26) | copy-start | bytes 292
  7.2 14.9 %copy-start.30 = (bf16[64]{0:T(256)(128)(2,1)S(1)}, bf16[64]{0:T(256)(128)(2,1)}, u32[]{:S(2)}) copy-start(bf16[64]{0:T(256)(128)(2,1)} %param.30) | copy-start | bytes 388
  7.2 57.7 %all-gather.10.cloned.1.call-start = ((), (), s32[]{:S(2)}) async-start(), calls=%async_computation.8 | async-start | bytes 3342336 | tf_op jit(solution)/shard_map/all_gather | solution.py:177
  8.0 148.3 %all-gather.8.cloned.1.call-start = ((), (), s32[]{:S(2)}) async-start(), calls=%async_computation.7 | async-start | bytes 4718592 | tf_op jit(solution)/shard_map/all_gather | solution.py:173
  16.4 185.2 %all-gather.12.cloned.1.call-start = ((), (), s32[]{:S(2)}) async-start(), calls=%async_computation.9 | async-start | bytes 1114112 | tf_op jit(solution)/shard_map/all_gather | solution.py:181
  17.2 276.4 %all-gather.20.cloned.1.call-start = ((), (), s32[]{:S(2)}) async-start(), calls=%async_computation.14 | async-start | bytes 4718592 | tf_op jit(solution)/shard_map/all_gather | solution.py:213
  17.7 368.7 %all-gather.14.cloned.1.call-start = ((), (), s32[]{:S(2)}) async-start(), calls=%async_computation.10 | async-start | bytes 4718592 | tf_op jit(solution)/shard_map/all_gather | solution.py:174
  18.3 426.0 %all-gather.16.cloned.1.call-start = ((), (), s32[]{:S(2)}) async-start(), calls=%async_computation.11 | async-start | bytes 4456448 | tf_op jit(solution)/shard_map/all_gather | solution.py:179
  18.9 482.2 %all-gather.18.cloned.1.call-start = ((), (), s32[]{:S(2)}) async-start(), calls=%async_computation.12 | async-start | bytes 4456448 | tf_op jit(solution)/shard_map/all_gather | solution.py:182
  19.6 562.3 %reduce-scatter.22.cloned.1.call-start = ((), (), s32[]{:S(2)}) async-start(), calls=%async_computation.19 | async-start | bytes 1114112
  339.2 307.7 %reduce-scatter.18.cloned.1.call-start = ((), (), s32[]{:S(2)}) async-start(), calls=%async_computation.17 | async-start | bytes 3342336 | tf_op jit(solution)/shard_map/reduce_scatter | solution.py:242
  350.2 380.2 %reduce-scatter.24.cloned.1.call-start = ((), (), s32[]{:S(2)}) async-start(), calls=%async_computation.20 | async-start | bytes 4456448
  468.7 345.1 %reduce-scatter.20.cloned.1.call-start = ((), (), s32[]{:S(2)}) async-start(), calls=%async_computation.18 | async-start | bytes 4456448 | tf_op jit(solution)/shard_map/reduce_scatter | solution.py:248
  518.7 389.0 %reduce-scatter.16.cloned.1.call-start = ((), (), s32[]{:S(2)}) async-start(), calls=%async_computation.16 | async-start | bytes 4718592 | tf_op jit(solution)/shard_map/reduce_scatter | solution.py:262
  525.8 475.8 %reduce-scatter.14.cloned.1.call-start = ((), (), s32[]{:S(2)}) async-start(), calls=%async_computation.15 | async-start | bytes 4718592 | tf_op jit(solution)/shard_map/reduce_scatter | solution.py:265
  535.7 559.5 %reduce-scatter.12.cloned.1.call-start = ((), (), s32[]{:S(2)}) async-start(), calls=%async_computation.13 | async-start | bytes 4718592 | tf_op jit(solution)/shard_map/reduce_scatter | solution.py:201
  546.4 455.1 %copy-start = (bf16[128,2048]{1,0:T(8,128)(2,1)S(1)}, bf16[128,2048]{1,0:T(8,128)(2,1)}, u32[]{:S(2)}) copy-start(bf16[128,2048]{1,0:T(8,128)(2,1)} %param.19) | copy-start | bytes 1572868
  546.4 455.1 %copy-start.12 = (f32[2048]{0:T(1024)S(1)}, f32[2048]{0:T(1024)}, u32[]{:S(2)}) copy-start(f32[2048]{0:T(1024)} %copy-done.11) | copy-start | bytes 24580
  546.4 455.1 %copy-start.14 = (f32[2048]{0:T(1024)S(1)}, f32[2048]{0:T(1024)}, u32[]{:S(2)}) copy-start(f32[2048]{0:T(1024)} %copy-done.13) | copy-start | bytes 24580
  546.5 455.1 %copy-start.16 = (f32[128]{0:T(128)S(1)}, f32[128]{0:T(128)}, u32[]{:S(2)}) copy-start(f32[128]{0:T(128)} %copy-done.15) | copy-start | bytes 1540
  546.5 457.0 %copy-start.24 = (f32[128]{0:T(128)S(1)}, f32[128]{0:T(128)}, u32[]{:S(2)}) copy-start(f32[128]{0:T(128)} %copy-done.23) | copy-start | bytes 1540
  546.5 457.0 %copy-start.19 = (f32[128]{0:T(128)S(1)}, f32[128]{0:T(128)}, u32[]{:S(2)}) copy-start(f32[128]{0:T(128)} %copy-done.18) | copy-start | bytes 1540
  546.5 548.7 %copy-start.5 = (bf16[128,2048]{1,0:T(8,128)(2,1)S(1)}, bf16[128,2048]{1,0:T(8,128)(2,1)}, u32[]{:S(2)}) copy-start(bf16[128,2048]{1,0:T(8,128)(2,1)} %param.33) | copy-start | bytes 1572868
  (30 other events, 105.1 us)
Sparse Core Ops, SparseCore 0:
  10.5 54.3 all-gather.9
  67.2 89.0 all-gather.7
  158.5 43.0 all-gather.11
  203.1 90.3 all-gather.19
  295.6 90.8 all-gather.13
  388.7 55.5 all-gather.15
  446.6 54.4 all-gather.17
  504.9 62.2 reduce-scatter.21
  571.8 75.0 reduce-scatter.17
  651.3 79.0 reduce-scatter.23
  734.4 79.3 reduce-scatter.19
  816.2 91.4 reduce-scatter.15
  910.3 91.2 reduce-scatter.13
  1004.0 91.2 reduce-scatter.11
where the time goes:
time: 1180 us; the launch traced here: 1170 us
  waiting for transfers between devices  856 us (73%)
  blocking collectives  132 us (11%)
  matrix products  91.6 us (8%)
  local copies, waits for them, and re-layouts  34.4 us (3%)
  other arithmetic  29.9 us (3%)
  between operations  17.5 us (1%)
    reduce_scatter x1, waiting for transfers between devices, shards(): lax.psum_scatter(d_second.astype(jnp.bfloat16), 'col', scatter_dimension=...  93.8 us
    reduce_scatter x1, waiting for transfers between devices, shards(): lax.psum_scatter(d_first.astype(jnp.bfloat16), 'col', scatter_dimension=0...  92.1 us
    all_gather x1, waiting for transfers between devices, shards(): grad_rows = lax.all_gather(cotangent, 'col', axis=0, tiled=True)  91.9 us
    all_gather x1, waiting for transfers between devices, shards(): lax.all_gather(normed[0].astype(jnp.bfloat16), 'col', axis=0, tiled=True)  91.3 us
    reduce_scatter x1, waiting for transfers between devices, shards(): lax.psum_scatter((jnp.dot(attended, dense_full, preferred_element_type=jn...  89.6 us
    unnamed x16, waiting for transfers between devices  85.6 us
    reduce_scatter x1, waiting for transfers between devices, shards(): lax.psum_scatter(up_grad.astype(jnp.bfloat16), 'row', scatter_dimension=0...  81.4 us
    unnamed x2, blocking collectives  67.2 us
  transfers between devices with their start and end apart: 14, of which 13 were waited for; matrix products, arithmetic and copies ran while one was open for 12% of the time, Pallas kernels for 0%

commit v1 on v0

v1 whole, which is shorter than its diff:
```python
import functools
import itertools
import math

import jax
import jax.numpy as jnp
from jax import lax
from jax.experimental import pallas as pl
from jax.experimental.pallas import tpu as pltpu
from jax.sharding import Mesh
from jax.sharding import PartitionSpec as P

HS = 256
ROT = 64
BLOCK = 256
SIZES = {"xh": 2, "y": 4, "c": 2, "z": 4, "xl": 2}
NAMES = tuple(SIZES)
ROW = ("xh", "y", "c")
COL = ("z", "xl")
F32 = jnp.float32
BF16 = jnp.bfloat16


def hop(value, **deltas):
    axes = tuple(name for name in NAMES if name in deltas)

    def flat(coords):
        index = 0
        for name, place in zip(axes, coords):
            index = index * SIZES[name] + place % SIZES[name]
        return index

    pairs = []
    for coords in itertools.product(*[range(SIZES[name]) for name in axes]):
        moved = [place + deltas[name] for name, place in zip(axes, coords)]
        pairs.append((flat(coords), flat(moved)))
    return lax.ppermute(value, axes if len(axes) > 1 else axes[0], pairs)


def put(buffer, piece, start):
    return lax.dynamic_update_slice_in_dim(buffer, piece, start, 0)


def rows_at(value, start, count):
    return lax.dynamic_slice_in_dim(value, start, count, 0)


def gather_col(piece):
    z, xl = lax.axis_index("z"), lax.axis_index("xl")
    count, width = piece.shape
    other = hop(piece, xl=1)
    pair = jnp.zeros((2 * count, width), piece.dtype)
    pair = put(put(pair, piece, xl * count), other, (1 - xl) * count)
    back = hop(pair, z=1)
    ahead = hop(pair, z=3)
    far_low = hop(back[:count], z=1)
    far_high = hop(ahead[count:], z=3)
    whole = jnp.zeros((8 * count, width), piece.dtype)
    whole = put(whole, pair, z * 2 * count)
    whole = put(whole, back, (z + 3) % 4 * 2 * count)
    whole = put(whole, ahead, (z + 1) % 4 * 2 * count)
    whole = put(whole, far_low, (z + 2) % 4 * 2 * count)
    return put(whole, far_high, (z + 2) % 4 * 2 * count + count)


def scatter_col(whole):
    z, xl = lax.axis_index("z"), lax.axis_index("xl")
    count = whole.shape[0] // 8
    far = rows_at(whole, (z + 2) % 4 * 2 * count, 2 * count)
    up = rows_at(whole, (z + 1) % 4 * 2 * count, 2 * count)
    down = rows_at(whole, (z + 3) % 4 * 2 * count, 2 * count)
    own = rows_at(whole, z * 2 * count, 2 * count)
    low = hop(far[:count], z=1)
    high = hop(far[count:], z=3)
    up = jnp.concatenate([up[:count] + low, up[count:]], 0)
    down = jnp.concatenate([down[:count], down[count:] + high], 0)
    from_back = hop(up, z=1)
    from_ahead = hop(down, z=3)
    total = own.astype(F32) + from_back.astype(F32) + from_ahead.astype(F32)
    sent = rows_at(total, (1 - xl) * count, count).astype(BF16)
    return rows_at(total, xl * count, count) + hop(sent, xl=1).astype(F32)


def gather_row(piece):
    y = lax.axis_index("y")
    count, width = piece.shape
    pair = jnp.concatenate([piece, hop(piece, xh=1)], 0)
    half = jnp.zeros((8 * count, width), piece.dtype)
    half = put(half, pair, y * 2 * count)
    for step in (1, 3, 2):
        half = put(half, hop(pair, y=step), (y - step + 4) % 4 * 2 * count)
    return jnp.concatenate([half, hop(half, c=1)], 0)


def scatter_row(whole):
    y = lax.axis_index("y")
    count = whole.shape[0] // 16
    half = whole[: 8 * count].astype(F32) + hop(whole[8 * count :], c=1).astype(F32)
    half = half.astype(BF16)
    pair = rows_at(half, y * 2 * count, 2 * count).astype(F32)
    for step in (1, 3, 2):
        pair = pair + hop(
            rows_at(half, (y + step) % 4 * 2 * count, 2 * count), y=step
        ).astype(F32)
    return pair[:count] + hop(pair[count:].astype(BF16), xh=1).astype(F32)


def sum_row(value):
    value = value + hop(value, c=1)
    value = value + hop(value, xh=1)
    return value + hop(value, y=1) + hop(value, y=2) + hop(value, y=3)


def sum_col(value):
    value = value + hop(value, xl=1)
    return value + hop(value, z=1) + hop(value, z=2) + hop(value, z=3)


def flips(view):
    core, xh = lax.axis_index("c"), lax.axis_index("xh")
    view = jnp.where(core == 1, view[:, ::-1], view)
    return jnp.where(xh == 1, view[:, :, :, ::-1], view)


def to_own_order(value):
    rows, width = value.shape
    view = value.reshape(rows, 2, 4, 2, width // 16).transpose(0, 3, 2, 1, 4)
    return flips(view).reshape(rows, width)


def from_own_order(value):
    rows, width = value.shape
    view = flips(value.reshape(rows, 2, 4, 2, width // 16))
    return view.transpose(0, 3, 2, 1, 4).reshape(rows, width)


def nt(left, right):
    return lax.dot_general(left, right, (((1,), (1,)), ((), ())), preferred_element_type=F32)


def tn(left, right):
    return lax.dot_general(left, right, (((0,), (0,)), ((), ())), preferred_element_type=F32)


def nn(left, right):
    return jnp.dot(left, right, preferred_element_type=F32)


def turn(part, cosine, sine):
    lane = lax.broadcasted_iota(jnp.int32, part.shape, 1)
    ahead = pltpu.roll(part, 128 - ROT // 2, 1)
    behind = pltpu.roll(part, ROT // 2, 1)
    return part * cosine + jnp.where(lane < ROT // 2, ahead, behind) * sine


def block_allowed(doc_col, doc_row, start, width):
    docs = doc_col[start : start + BLOCK] == doc_row[:, :width]
    row = start + lax.broadcasted_iota(jnp.int32, (BLOCK, width), 0)
    column = lax.broadcasted_iota(jnp.int32, (BLOCK, width), 1)
    return docs & (column <= row)


def attend_kernel(mix_ref, bias_ref, cos_ref, sin_ref, doc_col_ref, doc_row_ref, qkv_ref, out_ref, log_ref):
    rows = mix_ref.shape[0]
    for start in range(0, rows, BLOCK):
        at = pl.ds(start, BLOCK)
        cosine, sine = cos_ref[at, :], sin_ref[at, :]
        for first in (0, HS):
            head = mix_ref[at, first : first + 128] + bias_ref[:, first : first + 128]
            qkv_ref[at, first : first + 128] = turn(head, cosine, sine).astype(BF16)
            rest = mix_ref[at, first + 128 : first + HS] + bias_ref[:, first + 128 : first + HS]
            qkv_ref[at, first + 128 : first + HS] = rest.astype(BF16)
        qkv_ref[at, 2 * HS :] = (mix_ref[at, 2 * HS :] + bias_ref[:, 2 * HS :]).astype(BF16)
    doc_row = doc_row_ref[...]
    doc_col = doc_col_ref[...]
    for start in range(0, rows, BLOCK):
        width = start + BLOCK
        at = pl.ds(start, BLOCK)
        scores = nt(qkv_ref[at, :HS], qkv_ref[:width, HS : 2 * HS]) * HS ** (-0.5)
        scores = jnp.where(block_allowed(doc_col, doc_row, start, width), scores, -1e30)
        top = jnp.max(scores, axis=1, keepdims=True)
        raised = jnp.exp(scores - top)
        total = jnp.sum(raised, axis=1, keepdims=True)
        probabilities = (raised * (1.0 / total)).astype(BF16)
        out_ref[at, :] = nn(probabilities, qkv_ref[:width, 2 * HS :]).astype(BF16)
        log_ref[at, :] = top + jnp.log(total)


def attend_back_kernel(qkv_ref, grad_ref, log_ref, cos_ref, sin_ref, doc_col_ref, doc_row_ref, out_ref, sum_ref, dk_ref, dv_ref):
    rows = qkv_ref.shape[0]
    scaling = HS ** (-0.5)
    doc_row = doc_row_ref[...]
    doc_col = doc_col_ref[...]
    sums = [jnp.zeros((1, HS), F32) for _ in range(3)]

    def finish(value, start, first):
        at = pl.ds(start, BLOCK)
        head = turn(value[:, :128], cos_ref[at, :], -sin_ref[at, :]).astype(BF16)
        rest = value[:, 128:].astype(BF16)
        out_ref[at, first : first + 128] = head
        out_ref[at, first + 128 : first + HS] = rest
        both = jnp.concatenate([head.astype(F32), rest.astype(F32)], 1)
        return jnp.sum(both, axis=0, keepdims=True)

    for start in range(0, rows, BLOCK):
        width = start + BLOCK
        at = pl.ds(start, BLOCK)
        query = qkv_ref[at, :HS]
        grad = grad_ref[at, :]
        scores = nt(query, qkv_ref[:width, HS : 2 * HS]) * scaling
        allowed = block_allowed(doc_col, doc_row, start, width)
        weights = jnp.where(allowed, jnp.exp(scores - log_ref[at, :]), 0.0)
        probabilities = weights.astype(BF16)
        d_probs = nt(grad, qkv_ref[:width, 2 * HS :])
        inner = jnp.sum(weights * d_probs, axis=1, keepdims=True)
        d_scores = (weights * (d_probs - inner)).astype(BF16)
        d_values = tn(probabilities, grad)
        d_keys = tn(d_scores, query) * scaling
        if start:
            dv_ref[:start, :] += d_values[:start]
            dk_ref[:start, :] += d_keys[:start]
        dv_ref[start:width, :] = d_values[start:]
        dk_ref[start:width, :] = d_keys[start:]
        d_query = nn(d_scores, qkv_ref[:width, HS : 2 * HS]) * scaling
        sums[0] = sums[0] + finish(d_query, start, 0)
    for start in range(0, rows, BLOCK):
        at = pl.ds(start, BLOCK)
        sums[1] = sums[1] + finish(dk_ref[at, :], start, HS)
        values = dv_ref[at, :].astype(BF16)
        out_ref[at, 2 * HS :] = values
        sums[2] = sums[2] + jnp.sum(values.astype(F32), axis=0, keepdims=True)
    for part in range(3):
        sum_ref[:, part * HS : (part + 1) * HS] = sums[part]


def vmem_call(kernel, outs, args, scratch=(), flops=0, transcendentals=0):
    spec = pl.BlockSpec(memory_space=pltpu.VMEM)
    moved = sum(math.prod(a.shape) * a.dtype.itemsize for a in (*outs, *args))
    return pl.pallas_call(
        kernel,
        out_shape=outs,
        in_specs=[spec] * len(args),
        out_specs=[spec] * len(outs),
        scratch_shapes=scratch,
        compiler_params=pltpu.CompilerParams(vmem_limit_bytes=40 * 1024 * 1024),
        cost_estimate=pl.CostEstimate(
            flops=flops, bytes_accessed=moved, transcendentals=transcendentals
        ),
    )(*args)


def shape(rows, columns, dtype):
    return jax.ShapeDtypeStruct((rows, columns), dtype)


def attend(mix, bias, cosine, sine, doc_col, doc_row):
    rows = mix.shape[0]
    outs = (shape(rows, 3 * HS, BF16), shape(rows, HS, BF16), shape(rows, 1, F32))
    return vmem_call(
        attend_kernel,
        outs,
        (mix, bias, cosine, sine, doc_col, doc_row),
        flops=4 * rows * rows * HS,
        transcendentals=rows * rows,
    )


def attend_back(qkv, grad, logs, cosine, sine, doc_col, doc_row):
    rows = qkv.shape[0]
    outs = (shape(rows, 3 * HS, BF16), shape(1, 3 * HS, F32))
    return vmem_call(
        attend_back_kernel,
        outs,
        (qkv, grad, logs, cosine, sine, doc_col, doc_row),
        scratch=[pltpu.VMEM((rows, HS), F32), pltpu.VMEM((rows, HS), F32)],
        flops=10 * rows * rows * HS,
        transcendentals=rows * rows,
    )


def doc_layout(lengths, row_count):
    ends = jnp.cumsum(lengths, dtype=jnp.int32)
    places = jnp.arange(row_count, dtype=jnp.int32)
    passed = places[:, None] >= ends[None, :]
    doc_ids = jnp.sum(passed.astype(jnp.int32), axis=1, dtype=jnp.int32)
    begins = jnp.sum(jnp.where(passed, lengths[None, :], 0), axis=1, dtype=jnp.int32)
    return (doc_ids, places - begins)


def rotary_tables(positions):
    half = ROT // 2
    lane = jnp.arange(128, dtype=jnp.int32)
    frequency = 1.0 / 10000.0 ** ((lane % half).astype(F32) * (2.0 / ROT))
    frequency = jnp.where(lane < ROT, frequency, 0.0)
    angles = positions.astype(F32)[:, None] * frequency[None, :]
    sign = jnp.where(lane < half, -1.0, 1.0)
    return (jnp.cos(angles), jnp.sin(angles) * sign[None, :])


def gelu_pair(hidden):
    normal = 0.5 * (1.0 + lax.erf(hidden * (1.0 / math.sqrt(2.0))))
    density = jnp.exp(-0.5 * hidden * hidden) * (1.0 / math.sqrt(2.0 * math.pi))
    return (hidden * normal, normal + hidden * density)


def shards(
    tokens,
    doc_lengths,
    input_gain,
    input_shift,
    post_gain,
    post_shift,
    qkv_weight,
    qkv_bias,
    dense_weight,
    dense_bias,
    up_weight,
    up_bias,
    down_weight,
    down_bias,
    cotangent,
):
    row_index = (lax.axis_index("xh") * 4 + lax.axis_index("y")) * 2 + lax.axis_index("c")
    slice_rows = qkv_weight.shape[0]
    qkv_cols, up_cols = qkv_weight.shape[1], up_weight.shape[1]

    tok_rows = tokens.astype(F32)
    center = jnp.mean(tok_rows, axis=-1, keepdims=True)
    centered = tok_rows - center
    variance = jnp.mean(centered * centered, axis=-1, keepdims=True)
    inverse = lax.rsqrt(variance + 1e-05)
    normal_rows = to_own_order(centered * inverse)
    normal_all = gather_col(normal_rows.astype(BF16))

    def own_slice(vector):
        return rows_at(vector.astype(F32), row_index * slice_rows, slice_rows)[:, None]

    block_a = jnp.concatenate(
        [(qkv_weight.astype(F32) * own_slice(input_gain)).astype(BF16), dense_weight.T], 1
    )
    block_b = jnp.concatenate(
        [(up_weight.astype(F32) * own_slice(post_gain)).astype(BF16), down_weight.T], 1
    )
    full_a = gather_row(block_a)
    cot_rows = to_own_order(cotangent)
    cot_all = gather_col(cot_rows)
    full_b = gather_row(block_b)

    bias_part = jnp.pad(
        jnp.concatenate([qkv_bias, up_bias]).astype(F32)[None], ((0, 0), (0, 16))
    )
    bias_all = sum_row(
        jnp.where(jnp.arange(16)[:, None] == row_index, bias_part, 0.0)
    )
    qkv_bias_all = bias_all[:, : qkv_bias.shape[0]].reshape(1, qkv_cols)
    up_bias_all = bias_all[:, qkv_bias.shape[0] : qkv_bias.shape[0] + up_bias.shape[0]].reshape(
        1, up_cols
    )

    vectors = to_own_order(
        jnp.stack([input_gain, input_shift, post_gain, post_shift]).astype(F32)
    )
    gain_one, shift_one, gain_two, shift_two = (vectors[i : i + 1] for i in range(4))
    qkv_full, dense_full = full_a[:, :qkv_cols], full_a[:, qkv_cols:]
    up_full, down_full = full_b[:, :up_cols], full_b[:, up_cols:]
    ratio_one = jnp.broadcast_to((shift_one / gain_one).astype(BF16), (8, vectors.shape[1]))
    ratio_two = jnp.broadcast_to((shift_two / gain_two).astype(BF16), (8, vectors.shape[1]))
    qkv_bias_all = qkv_bias_all + nn(ratio_one, qkv_full)[:1]
    up_bias_all = up_bias_all + nn(ratio_two, up_full)[:1]

    row_count = normal_all.shape[0]
    doc_ids, positions = doc_layout(doc_lengths[0], row_count)
    cosine, sine = rotary_tables(positions)
    doc_col, doc_row = doc_ids[:, None], doc_ids[None, :]
    mixture = nn(normal_all, qkv_full)
    qkv, attended, logs = attend(mixture, qkv_bias_all, cosine, sine, doc_col, doc_row)
    hidden = nn(normal_all, up_full) + up_bias_all
    active, slope = gelu_pair(hidden)
    active = active.astype(BF16)
    slope = slope.astype(BF16)
    out_part = (nt(attended, dense_full) + nt(active, down_full)).astype(BF16)
    out_sum = scatter_col(out_part)

    d_attended = nn(cot_all, dense_full).astype(BF16)
    d_mixture, qkv_bias_part = attend_back(
        qkv, d_attended, logs, cosine, sine, doc_col, doc_row
    )
    d_hidden = (nn(cot_all, down_full) * slope.astype(F32)).astype(BF16)
    up_bias_part = jnp.sum(d_hidden.astype(F32), axis=0, keepdims=True)
    dense_part = tn(cot_all, attended).astype(BF16)
    down_part = tn(cot_all, active).astype(BF16)
    qkv_raw = tn(normal_all, d_mixture)
    up_raw = tn(normal_all, d_hidden)
    qkv_part = (qkv_raw * gain_one.T + shift_one.T * qkv_bias_part).astype(BF16)
    up_part = (up_raw * gain_two.T + shift_two.T * up_bias_part).astype(BF16)
    grad_a = scatter_row(jnp.concatenate([qkv_part, dense_part], 1))
    grad_b = scatter_row(jnp.concatenate([up_part, down_part], 1))
    u_part = (nt(d_mixture, qkv_full) + nt(d_hidden, up_full)).astype(BF16)
    u_rows = scatter_col(u_part)

    def against(weights, raw, bias_part, gain):
        wide = weights.astype(F32)
        return (
            (jnp.sum(wide * raw, axis=1) / gain[0])[None],
            (jnp.sum(wide * bias_part, axis=1) / gain[0])[None],
        )

    gain_one_part, shift_one_part = against(qkv_full, qkv_raw, qkv_bias_part, gain_one)
    gain_two_part, shift_two_part = against(up_full, up_raw, up_bias_part, gain_two)
    width = vectors.shape[1]
    small = jnp.concatenate(
        [
            gain_one_part,
            shift_one_part,
            gain_two_part,
            shift_two_part,
            jnp.sum(cot_rows.astype(F32), axis=0, keepdims=True),
        ],
        0,
    )
    biases = jnp.concatenate([qkv_bias_part, up_bias_part], 1)
    biases = jnp.pad(biases, ((0, 0), (0, width - biases.shape[1])))
    packed = jnp.concatenate([from_own_order(small), biases, jnp.zeros((2, width), F32)], 0)
    packed = sum_row(packed)
    qkv_bias_total = lax.dynamic_slice_in_dim(
        packed[5], row_index * qkv_bias.shape[0], qkv_bias.shape[0], 0
    )
    up_bias_total = lax.dynamic_slice_in_dim(
        packed[5], qkv_cols + row_index * up_bias.shape[0], up_bias.shape[0], 0
    )
    packed = sum_col(packed)

    layer_out = (
        tok_rows
        + from_own_order(out_sum)
        + dense_bias.astype(F32)
        + down_bias.astype(F32)
    ).astype(BF16)
    u_mean = jnp.mean(u_rows, axis=-1, keepdims=True)
    un_mean = jnp.mean(u_rows * normal_rows, axis=-1, keepdims=True)
    d_tokens = (u_rows - u_mean - normal_rows * un_mean) * inverse
    input_grad = (cotangent.astype(F32) + from_own_order(d_tokens)).astype(BF16)
    return (
        layer_out,
        input_grad,
        packed[0],
        packed[1],
        packed[2],
        packed[3],
        grad_a[:, :qkv_cols],
        qkv_bias_total,
        grad_a[:, qkv_cols:].T,
        packed[4],
        grad_b[:, :up_cols],
        up_bias_total,
        grad_b[:, up_cols:].T,
        packed[4],
    )


def solution(mesh):
    fine = Mesh(mesh.devices.reshape(tuple(SIZES.values())), NAMES)
    everywhere = P(ROW + COL, None)
    return jax.shard_map(
        shards,
        mesh=fine,
        in_specs=(
            everywhere,
            P(ROW, None),
            P(),
            P(),
            P(),
            P(),
            P(ROW, COL),
            P(COL + ROW),
            P(COL, ROW),
            P(),
            P(ROW, COL),
            P(COL + ROW),
            P(COL, ROW),
            P(),
            everywhere,
        ),
        out_specs=(
            everywhere,
            everywhere,
            P(),
            P(),
            P(),
            P(),
            P(ROW, COL),
            P(COL + ROW),
            P(COL, ROW),
            P(),
            P(ROW, COL),
            P(COL + ROW),
            P(COL, ROW),
            P(),
        ),
        check_vma=False,
    )
```

time: 1180 us -> 485 us (0.41)
  waiting for transfers between devices: 856 us -> 188 us
  blocking collectives: 132 us -> 0 us
  starting transfers between devices: 1.2 us -> 76.2 us
  local copies, waits for them, and re-layouts: 34.4 us -> 73.5 us
  other arithmetic: 29.9 us -> 59.1 us
  matrix products: 91.6 us -> 71.3 us
  between operations: 17.5 us -> 2.24 us
    reduce_scatter x5 -> x0, waiting for transfers between devices: 420 us -> none  [the longest x1 93.8 us: shards(): lax.psum_scatter(d_second.astype(jnp.bfloat16), 'col', scatter_dimension=...]
    all_gather x7 -> x0, waiting for transfers between devices: 350 us -> none  [the longest x1 91.9 us: shards(): grad_rows = lax.all_gather(cotangent, 'col', axis=0, tiled=True)]
    ppermute x0 -> x54, waiting for transfers between devices: none -> 188 us  [hop(): return lax.ppermute(value, axes if len(axes) > 1 else axes[0], pairs)]
    unnamed x16 -> x0, waiting for transfers between devices: 85.6 us -> none
    ppermute x0 -> x54, starting transfers between devices: none -> 76.2 us  [hop(): return lax.ppermute(value, axes if len(axes) > 1 else axes[0], pairs)]
    unnamed x2 -> x0, blocking collectives: 67.2 us -> none
    psum x1 -> x0, blocking collectives: 65.3 us -> none  [shards(): lax.psum((gain_one, shift_one, gain_two, shift_two, bias_grad), ('row', '...]
    dot_general x26 -> x14, matrix products: 91.6 us -> 71.3 us  [the longest x4 27.9 us: tn(): lax.dot_general(left, right, (((0,), (0,)), ((), ())), preferred_element_...]
  transfers between devices with their start and end apart: 14 -> 54, of which waited for: 13 -> 31; matrix products, arithmetic and copies ran while one was open for 12% -> 28% of each run, Pallas kernels for 0% -> 1%
where the time goes in v1:
time: 485 us; the launch traced here: 477 us
  waiting for transfers between devices  188 us (39%)
  starting transfers between devices  76.2 us (16%)
  local copies, waits for them, and re-layouts  73.5 us (15%)
  matrix products  71.3 us (15%)
  other arithmetic  59.1 us (12%)
  Pallas kernels  6.2 us (1%)
    ppermute x54, waiting for transfers between devices, hop(): return lax.ppermute(value, axes if len(axes) > 1 else axes[0], pairs)  188 us
    ppermute x54, starting transfers between devices, hop(): return lax.ppermute(value, axes if len(axes) > 1 else axes[0], pairs)  76.2 us
    dot_general x4, matrix products, tn(): lax.dot_general(left, right, (((0,), (0,)), ((), ())), preferred_element_...  27.9 us
    dot_general x4, matrix products, nt(): lax.dot_general(left, right, (((1,), (1,)), ((), ())), preferred_element_...  24.2 us
    dot_general x6, matrix products, nn(): return jnp.dot(left, right, preferred_element_type=F32)  19.2 us
    rev x6, local copies, waits for them, and re-layouts, flips(): return jnp.where(xh == 1, view[:, :, :, ::-1], view)  15.2 us
    dynamic_update_slice x20, local copies, waits for them, and re-layouts, put(): return lax.dynamic_update_slice_in_dim(buffer, piece, start, 0)  13.5 us
    unnamed x95, local copies, waits for them, and re-layouts  13 us
  transfers between devices with their start and end apart: 54, of which 31 were waited for; matrix products, arithmetic and copies ran while one was open for 28% of the time, Pallas kernels for 1%

profile of v1, /device:TPU:1, one launch (start us, length us, event | category | flops | bytes accessed | tf_op | source)
XLA Modules:
  0.0 477.0 jit_solution(106894789696394660)
XLA Ops:
  60.4 10.7 %collective-permute-done.15 = bf16[128,2048]{0,1:T(8,128)(2,1)} collective-permute-done((bf16[128,2048]{0,1:T(8,128)(2,1)}, bf16[128,2048]{0,1:T(8,128)(2,1)}, u32[]{:S(2)}, u32[]{:S(2)}) %collective-permute-start.15) | collective-permute-done | bytes 524320 | tf_op jit(solution)/shard_map/ppermute | solution.py:37
  96.5 7.3 %collective-permute-done.16 = bf16[256,2048]{0,1:T(8,128)(2,1)S(1)} collective-permute-done((bf16[256,2048]{0,1:T(8,128)(2,1)}, bf16[256,2048]{0,1:T(8,128)(2,1)S(1)}, u32[]{:S(2)}, u32[]{:S(2)}) %collective-permute-start.16) | collective-permute-done | bytes 1048608 | tf_op jit(solution)/shard_map/ppermute | solution.py:37
  110.5 7.2 %collective-permute-done.26 = bf16[256,2048]{0,1:T(8,128)(2,1)S(1)} collective-permute-done((bf16[256,2048]{0,1:T(8,128)(2,1)S(1)}, bf16[256,2048]{0,1:T(8,128)(2,1)S(1)}, u32[]{:S(2)}, u32[]{:S(2)}) %collective-permute-start.26) | collective-permute-done | bytes 1048608 | tf_op jit(solution)/shard_map/ppermute | solution.py:37
  118.9 13.2 %collective-permute-done.27 = bf16[256,2048]{0,1:T(8,128)(2,1)S(1)} collective-permute-done((bf16[256,2048]{0,1:T(8,128)(2,1)S(1)}, bf16[256,2048]{0,1:T(8,128)(2,1)S(1)}, u32[]{:S(2)}, u32[]{:S(2)}) %collective-permute-start.27) | collective-permute-done | bytes 1048608 | tf_op jit(solution)/shard_map/ppermute | solution.py:37
  134.8 5.1 %collective-permute-done.28 = bf16[128,2048]{0,1:T(8,128)(2,1)S(1)} collective-permute-done((bf16[128,2048]{0,1:T(8,128)(2,1)S(1)}, bf16[128,2048]{0,1:T(8,128)(2,1)S(1)}, u32[]{:S(2)}, u32[]{:S(2)}) %collective-permute-start.28) | collective-permute-done | bytes 524320 | tf_op jit(solution)/shard_map/ppermute | solution.py:37
  142.6 11.0 %collective-permute-done.29 = bf16[128,2048]{0,1:T(8,128)(2,1)S(1)} collective-permute-done((bf16[128,2048]{0,1:T(8,128)(2,1)S(1)}, bf16[128,2048]{0,1:T(8,128)(2,1)S(1)}, u32[]{:S(2)}, u32[]{:S(2)}) %collective-permute-start.29) | collective-permute-done | bytes 524320 | tf_op jit(solution)/shard_map/ppermute | solution.py:37
  173.7 8.6 %fusion.3 = (f32[2048]{0:T(1024)S(1)}, f32[2048]{0:T(1024)S(1)}, bf16[2048,768]{0,1:T(8,128)(2,1)S(1)}) fusion(bf16[2048,768]{0,1:T(8,128)(2,1)} %copy-done.8, f32[768]{0:T(1024)S(1)} %reduce.1, f32[2048]{0:T(1024)S(1)} %bitcast.104, f32[2048]{0:T(1024)S(1)} %bitcast.102, bf16[1024,2048]{0,1:T(8,128)(2,1)} %copy-done.16, bf16[1024,768]{1,0:T(8,128)(2,1)} %copy-done), kind=kOutput, calls=%fused_computation.15 | convolution fusion | flops 3235377152 | bytes 12094464 | tf_op jit(solution)/shard_map/dot_general | solution.py:142
  182.6 6.1 %collective-permute-start.44 = (bf16[1024,1024]{0,1:T(8,128)(2,1)S(1)}, bf16[1024,1024]{0,1:T(8,128)(2,1)S(1)}, u32[]{:S(2)}, u32[]{:S(2)}) collective-permute-start(bf16[1024,1024]{0,1:T(8,128)(2,1)S(1)} %pad_maximum_fusion.2), channel_id=1, source_target_pairs={{0,8},{8,0},{1,9},{9,1},{2,10},{10,2},{3,11},{11,3},{4,12},{12,4},... | collective-permute-start | bytes 6291464 | tf_op jit(solution)/shard_map/ppermute | solution.py:37
  198.5 11.6 %collective-permute-done.45 = bf16[256,1024]{0,1:T(8,128)(2,1)} collective-permute-done((bf16[256,1024]{0,1:T(8,128)(2,1)S(1)}, bf16[256,1024]{0,1:T(8,128)(2,1)}, u32[]{:S(2)}, u32[]{:S(2)}) %collective-permute-start.45) | collective-permute-done | bytes 524320 | tf_op jit(solution)/shard_map/ppermute | solution.py:37
  210.1 10.1 %collective-permute-done.47 = bf16[256,1024]{0,1:T(8,128)(2,1)} collective-permute-done((bf16[256,1024]{0,1:T(8,128)(2,1)S(1)}, bf16[256,1024]{0,1:T(8,128)(2,1)}, u32[]{:S(2)}, u32[]{:S(2)}) %collective-permute-start.47) | collective-permute-done | bytes 524320 | tf_op jit(solution)/shard_map/ppermute | solution.py:37
  224.3 6.4 %collective-permute-done.48 = bf16[128,1024]{0,1:T(8,128)(2,1)S(1)} collective-permute-done((bf16[128,1024]{0,1:T(8,128)(2,1)S(1)}, bf16[128,1024]{0,1:T(8,128)(2,1)S(1)}, u32[]{:S(2)}, u32[]{:S(2)}) %collective-permute-start.48) | collective-permute-done | bytes 262176 | tf_op jit(solution)/shard_map/ppermute | solution.py:37
  235.8 4.6 fusion.36
  242.5 7.1 %convolution_convert_fusion = bf16[2048,1024]{0,1:T(8,128)(2,1)} fusion(bf16[1024,2048]{0,1:T(8,128)(2,1)S(1)} %copy-done.15, f32[1024,1024]{1,0:T(8,128)S(1)} %fusion.36, f32[1024]{0:T(1024)S(1)} %bitcast.115), kind=kOutput, calls=%fused_computation.36 | convolution fusion | flops 4303355904 | bytes 12587008 | tf_op jit(solution)/shard_map/dot_general | solution.py:142
  249.6 6.8 %fusion.19 = f32[1024,2048]{1,0:T(8,128)S(1)} fusion(bf16[1024,2048]{0,1:T(8,128)(2,1)} %collective-permute-done.19, bf16[1024,2048]{0,1:T(8,128)(2,1)} %constant_dynamic-update-slice_fusion.7, f32[1024,1024]{1,0:T(8,128)S(1)} %fusion.36, f32[1024]{0:T(1024)S(1)} %bitcast.116), kind=kOutput, calls=%fused_computation.82 | convolution fusion | flops 4309647360 | bytes 20975616 | tf_op jit(solution)/shard_map/dot_general | solution.py:138
  259.6 7.7 %convert_reduce_fusion = (f32[1024]{0:T(1024)S(1)}, bf16[1024,1024]{1,0:T(8,128)(2,1)S(1)}) fusion(f32[1024,1024]{1,0:T(8,128)S(1)} %fusion.36, f32[1024]{0:T(1024)S(1)} %bitcast.117, bf16[1024,2048]{0,1:T(8,128)(2,1)S(1)} %copy-done.15, bf16[1024,2048]{0,1:T(8,128)(2,1)} %collective-permute-done.19, bf16[1024,2048]{0,1:T(8,128)(2,1)} %constant_dynamic-update-slice_fusion.7), kind=kOutput, calls=%fused_computation.32 | convolution fusion | flops 4319083520 | bytes 18882560 | tf_op jit(solution)/shard_map/dot_general | solution.py:146
  267.3 6.8 %fusion.37 = f32[1024,2048]{1,0:T(8,128)} fusion(bf16[1024,1024]{1,0:T(8,128)(2,1)S(1)} %get-tuple-element.143, bf16[2048,1024]{0,1:T(8,128)(2,1)S(1)} %fusion.10), kind=kOutput, calls=%fused_computation.189 | convolution fusion | flops 4294967296 | bytes 14680064 | tf_op jit(solution)/shard_map/dot_general | solution.py:138
  274.1 9.9 %fusion.1 = (f32[2048]{0:T(1024)S(1)}, f32[2048]{0:T(1024)S(1)}, bf16[2048,1024]{0,1:T(8,128)(2,1)}) fusion(bf16[2048,1024]{0,1:T(8,128)(2,1)S(1)} %fusion.10, f32[1024]{0:T(1024)S(1)} %get-tuple-element.142, f32[2048]{0:T(1024)S(1)} %bitcast.100, f32[2048]{0:T(1024)S(1)} %bitcast.98, bf16[1024,2048]{0,1:T(8,128)(2,1)S(1)} %copy-done.17, ...), kind=kOutput, calls=%fused_computation.3 | convolution fusion | flops 4313837568 | bytes 14716928 | tf_op jit(solution)/shard_map/dot_general | solution.py:142
  290.9 7.4 %add_convert_fusion.2 = bf16[1024,2048]{1,0:T(8,128)(2,1)S(1)} fusion(f32[1024,2048]{1,0:T(8,128)} %fusion.37, bf16[1024,768]{1,0:T(8,128)(2,1)S(1)} %copy-done.1, bf16[2048,768]{0,1:T(8,128)(2,1)} %copy-done.8), kind=kOutput, calls=%fused_computation.10 | convolution fusion | flops 3225419776 | bytes 17301504 | tf_op jit(solution)/shard_map/dot_general | solution.py:138
  321.2 7.3 %collective-permute-start.49 = (bf16[1024,2048]{0,1:T(8,128)(2,1)}, bf16[1024,2048]{0,1:T(8,128)(2,1)}, u32[]{:S(2)}, u32[]{:S(2)}) collective-permute-start(bf16[1024,2048]{0,1:T(8,128)(2,1)} %pad_maximum_fusion), channel_id=1, source_target_pairs={{0,8},{8,0},{1,9},{9,1},{2,10},{10,2},{3,11},{11,3},{4,12},{12,4},... | collective-permute-start | bytes 12582920 | tf_op jit(solution)/shard_map/ppermute | solution.py:37
  334.4 20.1 %collective-permute-done.23 = bf16[256,2048]{1,0:T(8,128)(2,1)S(1)} collective-permute-done((bf16[256,2048]{1,0:T(8,128)(2,1)S(1)}, bf16[256,2048]{1,0:T(8,128)(2,1)S(1)}, u32[]{:S(2)}, u32[]{:S(2)}) %collective-permute-start.23) | collective-permute-done | bytes 1048608 | tf_op jit(solution)/shard_map/ppermute | solution.py:37
  357.9 19.1 %collective-permute-done.33 = bf16[256,2048]{1,0:T(8,128)(2,1)S(1)} collective-permute-done((bf16[256,2048]{1,0:T(8,128)(2,1)S(1)}, bf16[256,2048]{1,0:T(8,128)(2,1)S(1)}, u32[]{:S(2)}, u32[]{:S(2)}) %collective-permute-start.33) | collective-permute-done | bytes 1048608 | tf_op jit(solution)/shard_map/ppermute | solution.py:37
  388.6 6.1 %rev.41 = f32[128,2,4,2,128]{4,3,2,1,0:T(2,128)} reverse(f32[128,2,4,2,128]{4,3,2,1,0:T(2,128)} %reverse_select_fusion.1), dimensions={3} | reverse | bytes 2097152 | tf_op jit(solution)/shard_map/rev | solution.py:122
  418.3 14.8 %collective-permute-done.50 = bf16[256,2048]{0,1:T(8,128)(2,1)} collective-permute-done((bf16[256,2048]{0,1:T(8,128)(2,1)}, bf16[256,2048]{0,1:T(8,128)(2,1)}, u32[]{:S(2)}, u32[]{:S(2)}) %collective-permute-start.50) | collective-permute-done | bytes 1048608 | tf_op jit(solution)/shard_map/ppermute | solution.py:37
  433.2 20.4 %collective-permute-done.52 = bf16[256,2048]{0,1:T(8,128)(2,1)} collective-permute-done((bf16[256,2048]{0,1:T(8,128)(2,1)}, bf16[256,2048]{0,1:T(8,128)(2,1)}, u32[]{:S(2)}, u32[]{:S(2)}) %collective-permute-start.52) | collective-permute-done | bytes 1048608 | tf_op jit(solution)/shard_map/ppermute | solution.py:37
  (357 shorter events, 239.5 us)
Async XLA Ops:
  2.1 35.5 %collective-permute-start.10 = (f32[16,128]{1,0:T(8,128)}, f32[16,128]{1,0:T(8,128)}, u32[]{:S(2)}, u32[]{:S(2)}) collective-permute-start(f32[16,128]{1,0:T(8,128)} %broadcast_select_fusion.4), channel_id=1, source_target_pairs={{0,8},{8,0},{1,9},{9,1},{2,10},{10,2},{3,11},{11,3},{4,12},{12,4},... | collective-permute-start | bytes 24584 | tf_op jit(solution)/shard_map/ppermute | solution.py:37
  7.7 45.7 %collective-permute-start.5 = (bf16[128,1024]{0,1:T(8,128)(2,1)}, bf16[128,1024]{0,1:T(8,128)(2,1)}, u32[]{:S(2)}, u32[]{:S(2)}) collective-permute-start(bf16[128,1024]{0,1:T(8,128)(2,1)} %pad_maximum_fusion.13), channel_id=1, source_target_pairs={{0,64},{64,0},{1,65},{65,1},{2,66},{66,2},{3,67},{67,3},{4,68},{68... | collective-permute-start | bytes 786440 | tf_op jit(solution)/shard_map/ppermute | solution.py:37
  21.4 37.1 %collective-permute-start = (bf16[128,2048]{1,0:T(8,128)(2,1)S(1)}, bf16[128,2048]{1,0:T(8,128)(2,1)}, u32[]{:S(2)}, u32[]{:S(2)}) collective-permute-start(bf16[128,2048]{1,0:T(8,128)(2,1)S(1)} %convert_element_type.213), channel_id=1, source_target_pairs={{0,1},{1,0},{2,3},{3,2},{4,5},{5,4},{6,7},{7,6},{8,9},{9,8},{10,11... | collective-permute-start | bytes 1572872 | tf_op jit(solution)/shard_map/ppermute | solution.py:37
  47.3 31.4 %collective-permute-start.25 = (bf16[128,2048]{0,1:T(8,128)(2,1)}, bf16[128,2048]{0,1:T(8,128)(2,1)}, u32[]{:S(2)}, u32[]{:S(2)}) collective-permute-start(bf16[128,2048]{0,1:T(8,128)(2,1)} %bitcast.89), channel_id=1, source_target_pairs={{0,1},{1,0},{2,3},{3,2},{4,5},{5,4},{6,7},{7,6},{8,9},{9,8},{10,11... | collective-permute-start | bytes 1572872 | tf_op jit(solution)/shard_map/ppermute | solution.py:37
  57.5 26.0 %collective-permute-start.6 = (bf16[256,1024]{0,1:T(8,128)(2,1)}, bf16[256,1024]{0,1:T(8,128)(2,1)}, u32[]{:S(2)}, u32[]{:S(2)}) collective-permute-start(bf16[256,1024]{0,1:T(8,128)(2,1)} %get-tuple-element.128), channel_id=1, source_target_pairs={{0,16},{16,32},{32,48},{48,0},{1,17},{17,33},{33,49},{49,1},{2,18}... | collective-permute-start | bytes 1572872 | tf_op jit(solution)/shard_map/ppermute | solution.py:37
  58.5 30.6 %collective-permute-start.8 = (bf16[256,1024]{0,1:T(8,128)(2,1)}, bf16[256,1024]{0,1:T(8,128)(2,1)}, u32[]{:S(2)}, u32[]{:S(2)}) collective-permute-start(bf16[256,1024]{0,1:T(8,128)(2,1)} %get-tuple-element.128), channel_id=1, source_target_pairs={{0,32},{16,48},{32,0},{48,16},{1,33},{17,49},{33,1},{49,17},{2,34}... | collective-permute-start | bytes 1572872 | tf_op jit(solution)/shard_map/ppermute | solution.py:37
  78.7 25.2 %collective-permute-start.16 = (bf16[256,2048]{0,1:T(8,128)(2,1)}, bf16[256,2048]{0,1:T(8,128)(2,1)S(1)}, u32[]{:S(2)}, u32[]{:S(2)}) collective-permute-start(bf16[256,2048]{0,1:T(8,128)(2,1)} %get-tuple-element.126), channel_id=1, source_target_pairs={{0,16},{16,32},{32,48},{48,0},{1,17},{17,33},{33,49},{49,1},{2,18}... | collective-permute-start | bytes 3145736 | tf_op jit(solution)/shard_map/ppermute | solution.py:37
  81.5 26.6 %collective-permute-start.17 = (bf16[256,2048]{0,1:T(8,128)(2,1)}, bf16[256,2048]{0,1:T(8,128)(2,1)S(1)}, u32[]{:S(2)}, u32[]{:S(2)}) collective-permute-start(bf16[256,2048]{0,1:T(8,128)(2,1)} %get-tuple-element.126), channel_id=1, source_target_pairs={{0,48},{16,0},{32,16},{48,32},{1,49},{17,1},{33,17},{49,33},{2,50}... | collective-permute-start | bytes 3145736 | tf_op jit(solution)/shard_map/ppermute | solution.py:37
  83.6 34.1 %collective-permute-start.26 = (bf16[256,2048]{0,1:T(8,128)(2,1)S(1)}, bf16[256,2048]{0,1:T(8,128)(2,1)S(1)}, u32[]{:S(2)}, u32[]{:S(2)}) collective-permute-start(bf16[256,2048]{0,1:T(8,128)(2,1)S(1)} %constant_dynamic-update-slice_fusion.5), channel_id=1, source_target_pairs={{0,2},{2,4},{4,6},{6,0},{1,3},{3,5},{5,7},{7,1},{8,10},{10,12},{12... | collective-permute-start | bytes 3145736 | tf_op jit(solution)/shard_map/ppermute | solution.py:37
  89.2 28.8 %collective-permute-start.2 = (bf16[256,2048]{0,1:T(8,128)(2,1)S(1)}, bf16[256,2048]{0,1:T(8,128)(2,1)S(1)}, u32[]{:S(2)}, u32[]{:S(2)}) collective-permute-start(bf16[256,2048]{0,1:T(8,128)(2,1)S(1)} %constant_dynamic-update-slice_fusion.20), channel_id=1, source_target_pairs={{0,6},{2,0},{4,2},{6,4},{1,7},{3,1},{5,3},{7,5},{8,14},{10,8},{12,... | collective-permute-start | bytes 3145736 | tf_op jit(solution)/shard_map/ppermute | solution.py:37
  95.2 36.9 %collective-permute-start.27 = (bf16[256,2048]{0,1:T(8,128)(2,1)S(1)}, bf16[256,2048]{0,1:T(8,128)(2,1)S(1)}, u32[]{:S(2)}, u32[]{:S(2)}) collective-permute-start(bf16[256,2048]{0,1:T(8,128)(2,1)S(1)} %constant_dynamic-update-slice_fusion.5), channel_id=1, source_target_pairs={{0,6},{2,0},{4,2},{6,4},{1,7},{3,1},{5,3},{7,5},{8,14},{10,8},{12,... | collective-permute-start | bytes 3145736 | tf_op jit(solution)/shard_map/ppermute | solution.py:37
  103.9 50.0 %collective-permute-start.9 = (bf16[1024,1024]{0,1:T(8,128)(2,1)}, bf16[1024,1024]{0,1:T(8,128)(2,1)S(1)}, u32[]{:S(2)}, u32[]{:S(2)}) collective-permute-start(bf16[1024,1024]{0,1:T(8,128)(2,1)} %constant_dynamic-update-slice_fusion.11), channel_id=1, source_target_pairs={{0,8},{8,0},{1,9},{9,1},{2,10},{10,2},{3,11},{11,3},{4,12},{12,4},... | collective-permute-start | bytes 6291464 | tf_op jit(solution)/shard_map/ppermute | solution.py:37
  108.2 80.5 %collective-permute-start.18 = (bf16[256,2048]{0,1:T(8,128)(2,1)}, bf16[256,2048]{0,1:T(8,128)(2,1)}, u32[]{:S(2)}, u32[]{:S(2)}) collective-permute-start(bf16[256,2048]{0,1:T(8,128)(2,1)} %get-tuple-element.126), channel_id=1, source_target_pairs={{0,32},{16,48},{32,0},{48,16},{1,33},{17,49},{33,1},{49,17},{2,34}... | collective-permute-start | bytes 3145736 | tf_op jit(solution)/shard_map/ppermute | solution.py:37
  191.0 41.3 %collective-permute-start.19 = (bf16[1024,2048]{0,1:T(8,128)(2,1)}, bf16[1024,2048]{0,1:T(8,128)(2,1)}, u32[]{:S(2)}, u32[]{:S(2)}) collective-permute-start(bf16[1024,2048]{0,1:T(8,128)(2,1)} %constant_dynamic-update-slice_fusion.7), channel_id=1, source_target_pairs={{0,8},{8,0},{1,9},{9,1},{2,10},{10,2},{3,11},{11,3},{4,12},{12,4},... | collective-permute-start | bytes 12582920 | tf_op jit(solution)/shard_map/ppermute | solution.py:37
  195.4 24.7 %collective-permute-start.47 = (bf16[256,1024]{0,1:T(8,128)(2,1)S(1)}, bf16[256,1024]{0,1:T(8,128)(2,1)}, u32[]{:S(2)}, u32[]{:S(2)}) collective-permute-start(bf16[256,1024]{0,1:T(8,128)(2,1)S(1)} %get-tuple-element.122), channel_id=1, source_target_pairs={{0,32},{16,48},{32,0},{48,16},{1,33},{17,49},{33,1},{49,17},{2,34}... | collective-permute-start | bytes 1572872 | tf_op jit(solution)/shard_map/ppermute | solution.py:37
  288.2 40.3 %collective-permute-start.20 = (bf16[128,2048]{1,0:T(8,128)(2,1)S(1)}, bf16[128,2048]{1,0:T(8,128)(2,1)S(1)}, u32[]{:S(2)}, u32[]{:S(2)}) collective-permute-start(bf16[128,2048]{1,0:T(8,128)(2,1)S(1)} %get-tuple-element.119), channel_id=1, source_target_pairs={{0,2},{2,4},{4,6},{6,0},{1,3},{3,5},{5,7},{7,1},{8,10},{10,12},{12... | collective-permute-start | bytes 1572872 | tf_op jit(solution)/shard_map/ppermute | solution.py:37
  289.6 38.9 %collective-permute-start.22 = (bf16[128,2048]{1,0:T(8,128)(2,1)S(1)}, bf16[128,2048]{1,0:T(8,128)(2,1)S(1)}, u32[]{:S(2)}, u32[]{:S(2)}) collective-permute-start(bf16[128,2048]{1,0:T(8,128)(2,1)S(1)} %get-tuple-element.120), channel_id=1, source_target_pairs={{0,6},{2,0},{4,2},{6,4},{1,7},{3,1},{5,3},{7,5},{8,14},{10,8},{12,... | collective-permute-start | bytes 1572872 | tf_op jit(solution)/shard_map/ppermute | solution.py:37
  321.2 79.3 %collective-permute-start.49 = (bf16[1024,2048]{0,1:T(8,128)(2,1)}, bf16[1024,2048]{0,1:T(8,128)(2,1)}, u32[]{:S(2)}, u32[]{:S(2)}) collective-permute-start(bf16[1024,2048]{0,1:T(8,128)(2,1)} %pad_maximum_fusion), channel_id=1, source_target_pairs={{0,8},{8,0},{1,9},{9,1},{2,10},{10,2},{3,11},{11,3},{4,12},{12,4},... | collective-permute-start | bytes 12582920 | tf_op jit(solution)/shard_map/ppermute | solution.py:37
  329.2 25.3 %collective-permute-start.23 = (bf16[256,2048]{1,0:T(8,128)(2,1)S(1)}, bf16[256,2048]{1,0:T(8,128)(2,1)S(1)}, u32[]{:S(2)}, u32[]{:S(2)}) collective-permute-start(bf16[256,2048]{1,0:T(8,128)(2,1)S(1)} %pad_maximum_fusion.6), channel_id=1, source_target_pairs={{0,6},{2,0},{4,2},{6,4},{1,7},{3,1},{5,3},{7,5},{8,14},{10,8},{12,... | collective-permute-start | bytes 3145736 | tf_op jit(solution)/shard_map/ppermute | solution.py:37
  329.9 26.7 %collective-permute-start.21 = (bf16[256,2048]{1,0:T(8,128)(2,1)S(1)}, bf16[256,2048]{1,0:T(8,128)(2,1)S(1)}, u32[]{:S(2)}, u32[]{:S(2)}) collective-permute-start(bf16[256,2048]{1,0:T(8,128)(2,1)S(1)} %pad_maximum_fusion.5), channel_id=1, source_target_pairs={{0,2},{2,4},{4,6},{6,0},{1,3},{3,5},{5,7},{7,1},{8,10},{10,12},{12... | collective-permute-start | bytes 3145736 | tf_op jit(solution)/shard_map/ppermute | solution.py:37
  331.9 45.1 %collective-permute-start.33 = (bf16[256,2048]{1,0:T(8,128)(2,1)S(1)}, bf16[256,2048]{1,0:T(8,128)(2,1)S(1)}, u32[]{:S(2)}, u32[]{:S(2)}) collective-permute-start(bf16[256,2048]{1,0:T(8,128)(2,1)S(1)} %pad_maximum_fusion.8), channel_id=1, source_target_pairs={{0,6},{2,0},{4,2},{6,4},{1,7},{3,1},{5,3},{7,5},{8,14},{10,8},{12,... | collective-permute-start | bytes 3145736 | tf_op jit(solution)/shard_map/ppermute | solution.py:37
  333.7 45.3 %collective-permute-start.31 = (bf16[256,2048]{1,0:T(8,128)(2,1)S(1)}, bf16[256,2048]{1,0:T(8,128)(2,1)S(1)}, u32[]{:S(2)}, u32[]{:S(2)}) collective-permute-start(bf16[256,2048]{1,0:T(8,128)(2,1)S(1)} %pad_maximum_fusion.7), channel_id=1, source_target_pairs={{0,2},{2,4},{4,6},{6,0},{1,3},{3,5},{5,7},{7,1},{8,10},{10,12},{12... | collective-permute-start | bytes 3145736 | tf_op jit(solution)/shard_map/ppermute | solution.py:37
  408.5 45.0 %collective-permute-start.52 = (bf16[256,2048]{0,1:T(8,128)(2,1)}, bf16[256,2048]{0,1:T(8,128)(2,1)}, u32[]{:S(2)}, u32[]{:S(2)}) collective-permute-start(bf16[256,2048]{0,1:T(8,128)(2,1)} %get-tuple-element.107), channel_id=1, source_target_pairs={{0,32},{16,48},{32,0},{48,16},{1,33},{17,49},{33,1},{49,17},{2,34}... | collective-permute-start | bytes 3145736 | tf_op jit(solution)/shard_map/ppermute | solution.py:37
  410.1 47.0 %collective-permute-start.51 = (bf16[256,2048]{0,1:T(8,128)(2,1)}, bf16[256,2048]{0,1:T(8,128)(2,1)}, u32[]{:S(2)}, u32[]{:S(2)}) collective-permute-start(bf16[256,2048]{0,1:T(8,128)(2,1)} %get-tuple-element.108), channel_id=1, source_target_pairs={{0,48},{16,0},{32,16},{48,32},{1,49},{17,1},{33,17},{49,33},{2,50}... | collective-permute-start | bytes 3145736 | tf_op jit(solution)/shard_map/ppermute | solution.py:37
  (75 other events, 895.8 us)
